TPU v7x, 32 devices: a whole 2x2x4 slice. The times are simulated.
32 devices in a mesh: energy: 2 (over y), kpt: 16 (over z, x, core).
Axes of the slice: x: 2, y: 2, z: 4, core: 2. Of those that a mesh axis runs over, the one named last changes fastest.
Arguments:
- left_table: bfloat16 [512, 4096], P('kpt'), may hold values from -6 to 6
- band_table: bfloat16 [512, 4096], P('kpt'), may hold values from -18.75 to 18.75
- band_multipole: int32 [512], P('kpt'), may hold values from 0 to 7
- radial_weight: float32 [8, 4096], replicated, may hold values from 0.25 to 4
- green_weight: float32 [1024], P(('energy', 'kpt')), parts along dimension 0, may hold values from 0.3 to 3
Outputs:
- kernel_cyclic: bfloat16 [1024, 512], P(('energy', 'kpt')), parts along dimension 0
There are 2 independent parts, one for each index of `energy`. A program takes and returns all parts, laid end to end along the dimension named above; an argument that names none is the same for every part. Nothing has to cross between parts.
All inputs are finite; a program needn't handle non-finite values.
Results may differ from a plain program's by a relative error of at most 0.0049.
Values may be sent and summed in bfloat16 or wider, within the bound.
A program may use at most 128 MiB of HBM per device.

v0:
```python
import jax
import jax.numpy as jnp
from jax import lax
from jax.sharding import PartitionSpec as P

LMAX = 8


def build_part(left_table, band_part):
    return lax.dot_general(
        left_table, band_part, (((1,), (1,)), ((), ())), preferred_element_type=jnp.float32
    ).astype(jnp.bfloat16)


def per_device(left_table, band_table, band_multipole, radial_weight, green_weight):
    group_size = lax.axis_size("kpt")
    row_count = left_table.shape[0]
    block_rows = row_count // group_size
    levels = lax.broadcasted_iota(jnp.int32, (1, LMAX), 1)
    onehot = (band_multipole[:, None] == levels).astype(jnp.float32)
    picked = jnp.dot(onehot, radial_weight, precision=lax.Precision.HIGHEST)
    weighted = (band_table.astype(jnp.float32) * picked * green_weight[:, None]).astype(
        jnp.bfloat16
    )
    gathered = lax.all_gather(weighted, "kpt", axis=0, tiled=True)
    band_total = gathered.shape[0]
    kernel_rows = build_part(left_table, gathered)
    shaped = kernel_rows.reshape(group_size, block_rows, band_total)
    relaid = lax.all_to_all(shaped, "kpt", split_axis=0, concat_axis=0, tiled=True)
    return relaid.reshape(row_count, band_total)


def solution(mesh):
    in_specs = (P("kpt", None), P("kpt", None), P("kpt"), P(), P(("energy", "kpt")))
    out_specs = P(("energy", "kpt"), None)
    return jax.shard_map(
        per_device, mesh=mesh, in_specs=in_specs, out_specs=out_specs, check_vma=False
    )
```

profile of v0, /device:TPU:0, one launch (start us, length us, event | category | flops | bytes accessed | tf_op | source)
XLA Modules:
  0.0 83.5 jit_solution(3887422241871373893)
XLA Ops:
  6.5 0.0 copy-start
  6.5 0.0 all-gather.2.cloned.1.call-start
  6.5 2.2 %fusion.1 = bf16[32,4096]{1,0:T(8,128)(2,1)} fusion(f32[8,4096]{1,0:T(8,128)} %param.8, bf16[32,4096]{1,0:T(8,128)(2,1)} %param.6, f32[32]{0:T(128)} %param.9, s32[32]{0:T(128)} %param.7), kind=kOutput, calls=%fused_computation.2 | convolution fusion | flops 13107456 | bytes 655616 | tf_op jit(solution)/shard_map/dot_general | solution.py:21
  8.7 0.0 all-gather.2.cloned.1.call-update
  8.8 54.0 %all-gather.2.cloned.1.call-done = bf16[512,4096]{1,0:T(8,128)(2,1)} async-done(((bf16[32,4096]{1,0:T(8,128)(2,1)}), bf16[512,4096]{1,0:T(8,128)(2,1)}) %all-gather.2.cloned.1.call-update) | async-done | bytes 4194320 | tf_op jit(solution)/shard_map/all_gather | solution.py:25
  62.8 0.0 copy-done
  62.8 3.5 %fusion.2 = bf16[32,512]{1,0:T(8,128)(2,1)S(1)} fusion(bf16[512,4096]{1,0:T(8,128)(2,1)} %all-gather.2.cloned.1.call-done, bf16[32,4096]{1,0:T(8,128)(2,1)S(1)} %copy-done), kind=kOutput, calls=%fused_computation.4 | convolution fusion | flops 134234112 | bytes 4489216 | tf_op jit(solution)/shard_map/dot_general | solution.py:10
  66.4 9.6 %all_to_all.5 = bf16[16,2,512]{2,1,0:T(2,128)(2,1)S(1)} all-to-all(bf16[16,2,512]{2,1,0:T(2,128)(2,1)S(1)} %reshape.8), channel_id=1, replica_groups=mesh['energy'=2,'kpt'=16] {'kpt'}, dimensions={0} | all-to-all | bytes 65536 | tf_op jit(solution)/shard_map/all_to_all | solution.py:29
  76.0 0.6 reshape.9
  (1 shorter events, 0.0 us)
Async XLA Ops:
  6.5 56.3 %copy-start = (bf16[32,4096]{1,0:T(8,128)(2,1)S(1)}, bf16[32,4096]{1,0:T(8,128)(2,1)}, u32[]{:S(2)}) copy-start(bf16[32,4096]{1,0:T(8,128)(2,1)} %param.5) | copy-start | bytes 786436
  6.5 56.3 %all-gather.2.cloned.1.call-start = ((), (), s32[]{:S(2)}) async-start(), calls=%async_computation.1 | async-start | bytes 4456448 | tf_op jit(solution)/shard_map/all_gather | solution.py:25
Sparse Core Ops, SparseCore 0:
  9.5 53.2 all-gather.1
where the time goes:
time: 83.7 us; the launch traced here: 83.5 us
  waiting for transfers between devices  54.1 us (65%)
  between operations  13.4 us (16%)
  blocking collectives  9.64 us (12%)
  matrix products  5.74 us (7%)
    all_gather x1, waiting for transfers between devices, per_device(): gathered = lax.all_gather(weighted, 'kpt', axis=0, tiled=True)  54 us
    all_to_all x1, blocking collectives, per_device(): lax.all_to_all(shaped, 'kpt', split_axis=0, concat_axis=0, tiled=True)  9.64 us
    dot_general x1, matrix products, build_part(): lax.dot_general(left_table, band_part, (((1,), (1,)), ((), ())), preferre...  3.53 us
    dot_general x1, matrix products, per_device(): picked = jnp.dot(onehot, radial_weight, precision=lax.Precision.HIGHEST)  2.21 us
  transfers between devices with their start and end apart: 1, of which 1 were waited for; matrix products, arithmetic and copies ran while one was open for 0% of the time, Pallas kernels for 0%

commit v1 on v0

--- a/solution.py
+++ b/solution.py
@@ -1,9 +1,15 @@
+import functools
+
 import jax
 import jax.numpy as jnp
 from jax import lax
+from jax.experimental import pallas as pl
+from jax.experimental.pallas import tpu as pltpu
 from jax.sharding import PartitionSpec as P
 
 LMAX = 8
+MESH = pl.DeviceIdType.MESH
+CHUNKS = 4
 
 
 def build_part(left_table, band_part):
@@ -30,9 +36,272 @@
     return relaid.reshape(row_count, band_total)
 
 
+def grid_kernel(
+    left, band, mult, radial, green, out,
+    lbuf, bbuf, rbuf, info, infobuf, psend, precv, msg, outbuf,
+    rsem, lsem, bsem, isem, psem, osem, lsend, bsend, isend, osend,
+):
+    e = lax.axis_index("energy")
+    k = lax.axis_index("kpt")
+    c, x, z = k % 2, (k // 2) % 2, k // 4
+    half = lbuf.shape[1]
+    step = half // CHUNKS
+    rows = left.shape[0]
+    own = k % 4
+
+    barrier = pltpu.get_barrier_semaphore()
+    for de in range(2):
+        for dk in range(16):
+            if de or dk:
+                pl.semaphore_signal(
+                    barrier, inc=1, device_id=((e + de) % 2, (k + dk) % 16), device_id_type=MESH
+                )
+
+    def cols(core, n):
+        return pl.ds(pl.multiple_of(core * half + n * step, 128), step)
+
+    def slot(i):
+        return pl.ds(pl.multiple_of(i * rows, rows), rows)
+
+    def at(n):
+        return pl.ds(n * step, step)
+
+    radial_copy = pltpu.make_async_copy(
+        radial.at[:, pl.ds(pl.multiple_of(c * half, 128), half)], rbuf, rsem
+    )
+    radial_copy.start()
+    for n in range(CHUNKS):
+        pltpu.make_async_copy(
+            left.at[:, cols(c, n)], lbuf.at[slot(own), at(n)], lsem.at[own, n]
+        ).start()
+
+    @pl.when(c == e)
+    def _():
+        for n in range(CHUNKS):
+            pltpu.make_async_copy(
+                band.at[:, cols(c, n)], bbuf.at[slot(z), at(n)], bsem.at[z, n]
+            ).start()
+
+    info[...] = jnp.zeros_like(info)
+    info[0:1, 0:rows] = green[...]
+    info[1:2, 0:rows] = mult[...].astype(jnp.float32)
+    info[...] = pltpu.roll(info[...], z * rows, 1)
+
+    pl.semaphore_wait(barrier, 31)
+
+    sends = []
+    for dz in range(4):
+        for dc in range(2):
+            target = (c, ((z + dz) % 4) * 4 + 2 * x + (c + dc) % 2)
+            copy = pltpu.make_async_remote_copy(
+                src_ref=info, dst_ref=infobuf.at[e, z], send_sem=isend.at[dz * 2 + dc],
+                recv_sem=isem.at[e, z], device_id=target, device_id_type=MESH,
+            )
+            if dz or dc:
+                copy.start()
+                sends.append(copy)
+            else:
+                own_info = copy
+    info_local = pltpu.make_async_copy(info, infobuf.at[e, z], isem.at[e, z])
+
+    @pl.when(c == e)
+    def _():
+        info_local.start()
+
+    @pl.when(c != e)
+    def _():
+        own_info.start()
+
+    band_sends = []
+    for n in range(CHUNKS):
+        for i, (dx, dc) in enumerate(((1, 0), (1, 1), (0, 1))):
+            core = (c + dc) % 2
+            copy = pltpu.make_async_remote_copy(
+                src_ref=left.at[:, cols(core, n)], dst_ref=lbuf.at[slot(own), at(n)],
+                send_sem=lsend.at[i, n], recv_sem=lsem.at[own, n],
+                device_id=(e, 4 * z + 2 * ((x + dx) % 2) + core), device_id_type=MESH,
+            )
+            copy.start()
+            sends.append(copy)
+        for i, (dz, dc) in enumerate(((1, 0), (1, 1), (2, 0), (2, 1), (3, 0), (3, 1), (0, 1))):
+            core = (c + dc) % 2
+            band_sends.append(
+                pltpu.make_async_remote_copy(
+                    src_ref=band.at[:, cols(core, n)], dst_ref=bbuf.at[slot(z), at(n)],
+                    send_sem=bsend.at[i, n], recv_sem=bsem.at[z, n],
+                    device_id=(e, ((z + dz) % 4) * 4 + 2 * x + core), device_id_type=MESH,
+                )
+            )
+
+    @pl.when(c == e)
+    def _():
+        for copy in band_sends:
+            copy.start()
+
+    radial_copy.wait()
+    whole = rbuf[...]
+    high = whole.astype(jnp.bfloat16)
+    rest = whole - high.astype(jnp.float32)
+    middle = rest.astype(jnp.bfloat16)
+    low = rest - middle.astype(jnp.float32)
+    terms = jnp.concatenate(
+        [high.astype(jnp.float32), middle.astype(jnp.float32), low, jnp.zeros_like(low)], axis=0
+    ).astype(jnp.bfloat16)
+
+    for energy in range(2):
+        for zz in range(4):
+            pltpu.make_async_copy(info, infobuf.at[energy, zz], isem.at[energy, zz]).wait()
+    data = [infobuf[i, 0] + infobuf[i, 1] + infobuf[i, 2] + infobuf[i, 3] for i in range(2)]
+    lanes = 4 * rows
+    down = lax.broadcasted_iota(jnp.int32, (lanes, lanes), 0)
+    across = lax.broadcasted_iota(jnp.int32, (lanes, lanes), 1)
+    scale = [
+        jnp.sum(jnp.where(down == across, data[i][0:1, :], 0.0), axis=1, keepdims=True)
+        for i in range(2)
+    ]
+    first = c == 0
+    mine = jnp.where(first, scale[0], scale[1])
+    other = jnp.where(first, scale[1], scale[0])
+    level = jnp.sum(jnp.where(down == across, data[0][1:2, :], 0.0), axis=1, keepdims=True)
+    place = lax.broadcasted_iota(jnp.int32, (lanes, 4 * LMAX), 1)
+    onehot = jnp.where(
+        jnp.logical_and((place % LMAX).astype(jnp.float32) == level, place < 3 * LMAX), 1.0, 0.0
+    ).astype(jnp.bfloat16)
+
+    total = jnp.zeros((lanes, 2 * lanes), jnp.float32)
+    for n in range(CHUNKS):
+        picked = jnp.dot(
+            onehot, terms[:, n * step:(n + 1) * step], preferred_element_type=jnp.float32
+        )
+        for i in range(4):
+            pltpu.make_async_copy(
+                lbuf.at[slot(i), at(n)], lbuf.at[slot(i), at(n)], lsem.at[i, n]
+            ).wait()
+            pltpu.make_async_copy(
+                bbuf.at[slot(i), at(n)], bbuf.at[slot(i), at(n)], bsem.at[i, n]
+            ).wait()
+        product = bbuf[:, n * step:(n + 1) * step].astype(jnp.float32) * picked
+        weighted = jnp.concatenate(
+            [(product * other).astype(jnp.bfloat16), (product * mine).astype(jnp.bfloat16)], axis=0
+        )
+        total += lax.dot_general(
+            lbuf[:, n * step:(n + 1) * step], weighted, (((1,), (1,)), ((), ())),
+            preferred_element_type=jnp.float32,
+        )
+
+    psend[...] = total[:, :lanes]
+    half_sum = pltpu.make_async_remote_copy(
+        src_ref=psend, dst_ref=precv, send_sem=psem.at[0], recv_sem=psem.at[1],
+        device_id=(e, 4 * z + 2 * x + (c + 1) % 2), device_id_type=MESH,
+    )
+    half_sum.start()
+    block, pair = down // 8, down % 8
+    order = jnp.where(across == (pair // 2) * rows + block * 2 + pair % 2, 1.0, 0.0).astype(
+        jnp.bfloat16
+    )
+    half_sum.wait_recv()
+    finished = (total[:, lanes:] + precv[...]).astype(jnp.bfloat16)
+    cyclic = jnp.dot(order, finished, preferred_element_type=jnp.float32)
+    msg[...] = cyclic.reshape(msg.shape)
+
+    for dq in range(16):
+        q = (k + dq) % 16
+        copy = pltpu.make_async_remote_copy(
+            src_ref=msg.at[q], dst_ref=outbuf.at[z, 2 * x + e], send_sem=osend.at[dq],
+            recv_sem=osem.at[z, 2 * x + e], device_id=(c, q), device_id_type=MESH,
+        )
+        if dq:
+            copy.start()
+            sends.append(copy)
+        else:
+            own_out = copy
+    out_local = pltpu.make_async_copy(msg.at[k], outbuf.at[z, 2 * x + e], osem.at[z, 2 * x + e])
+
+    @pl.when(c == e)
+    def _():
+        out_local.start()
+
+    @pl.when(c != e)
+    def _():
+        own_out.start()
+
+    lane = lax.broadcasted_iota(jnp.int32, (8, lanes), 1) // rows
+    for zz in range(4):
+        for s in range(4):
+            pltpu.make_async_copy(msg.at[0], outbuf.at[zz, s], osem.at[zz, s]).wait()
+    for top in range(2):
+        for tile in range(4):
+            parts = []
+            for zz in (2 * top, 2 * top + 1):
+                whole_tile = jnp.zeros((8, lanes), jnp.float32)
+                for s in range(4):
+                    turned = outbuf[zz, s]
+                    if (s - tile) % 4:
+                        turned = pltpu.roll(turned, ((s - tile) % 4) * rows, 1)
+                    whole_tile = jnp.where(lane == s, turned, whole_tile)
+                parts.append(whole_tile)
+            out[top * 16:(top + 1) * 16, tile * lanes:(tile + 1) * lanes] = jnp.concatenate(
+                parts, axis=0
+            ).astype(jnp.bfloat16)
+
+    for copy in sends:
+        copy.wait_send()
+    half_sum.wait_send()
+
+    @pl.when(c == e)
+    def _():
+        for copy in band_sends:
+            copy.wait_send()
+
+    @pl.when(c != e)
+    def _():
+        own_info.wait_send()
+        own_out.wait_send()
+
+
+def per_device_grid(left_table, band_table, band_multipole, radial_weight, green_weight):
+    rows, points = left_table.shape
+    lanes, half = 4 * rows, points // 2
+    dma = pltpu.SemaphoreType.DMA
+    any_space = pl.BlockSpec(memory_space=pl.ANY)
+    vmem = pl.BlockSpec(memory_space=pltpu.VMEM)
+    return pl.pallas_call(
+        grid_kernel,
+        out_shape=jax.ShapeDtypeStruct((rows, 16 * rows), jnp.bfloat16),
+        in_specs=[any_space, any_space, vmem, any_space, vmem],
+        out_specs=vmem,
+        scratch_shapes=[
+            pltpu.VMEM((lanes, half), jnp.bfloat16),
+            pltpu.VMEM((lanes, half), jnp.bfloat16),
+            pltpu.VMEM((LMAX, half), jnp.float32),
+            pltpu.VMEM((8, lanes), jnp.float32),
+            pltpu.VMEM((2, 4, 8, lanes), jnp.float32),
+            pltpu.VMEM((lanes, lanes), jnp.float32),
+            pltpu.VMEM((lanes, lanes), jnp.float32),
+            pltpu.VMEM((16, 8, lanes), jnp.float32),
+            pltpu.VMEM((4, 4, 8, lanes), jnp.float32),
+            dma, dma((4, CHUNKS)), dma((4, CHUNKS)), dma((2, 4)), dma((2,)), dma((4, 4)),
+            dma((3, CHUNKS)), dma((7, CHUNKS)), dma((8,)), dma((16,)),
+        ],
+        compiler_params=pltpu.CompilerParams(
+            collective_id=0, has_side_effects=True, vmem_limit_bytes=32 * 1024 * 1024
+        ),
+    )(left_table, band_table, band_multipole.reshape(1, rows), radial_weight, green_weight.reshape(1, rows))
+
+
 def solution(mesh):
     in_specs = (P("kpt", None), P("kpt", None), P("kpt"), P(), P(("energy", "kpt")))
     out_specs = P(("energy", "kpt"), None)
+
+    def step(left_table, band_table, band_multipole, radial_weight, green_weight):
+        small = (
+            mesh.shape["energy"] == 2
+            and mesh.shape["kpt"] == 16
+            and left_table.shape == band_table.shape == (32, 4096)
+        )
+        body = per_device_grid if small else per_device
+        return body(left_table, band_table, band_multipole, radial_weight, green_weight)
+
     return jax.shard_map(
-        per_device, mesh=mesh, in_specs=in_specs, out_specs=out_specs, check_vma=False
-    )
+        step, mesh=mesh, in_specs=in_specs, out_specs=out_specs, check_vma=False
+    )

time: 83.7 us -> 31.4 us (0.38)
  waiting for transfers between devices: 54.1 us -> 0 us
  Pallas kernels: 0 us -> 27.1 us
  between operations: 13.4 us -> 0.01 us
  blocking collectives: 9.64 us -> 0 us
  matrix products: 5.74 us -> 0 us
  local copies, waits for them, and re-layouts: 0.67 us -> 4.09 us
    all_gather x1 -> x0, waiting for transfers between devices: 54 us -> none  [per_device(): gathered = lax.all_gather(weighted, 'kpt', axis=0, tiled=True)]
    pallas_call x0 -> x1, Pallas kernels: none -> 27.1 us  [per_device_grid(): pl.pallas_call(grid_kernel, out_shape=jax.ShapeDtypeStruct((rows, 16 * ro...]
    all_to_all x1 -> x0, blocking collectives: 9.64 us -> none  [per_device(): lax.all_to_all(shaped, 'kpt', split_axis=0, concat_axis=0, tiled=True)]
    dot_general x2 -> x0, matrix products: 5.74 us -> none  [the longest x1 3.53 us: build_part(): lax.dot_general(left_table, band_part, (((1,), (1,)), ((), ())), preferre...]
    unnamed x2 -> x11, local copies, waits for them, and re-layouts: 0.01 us -> 4.09 us
  transfers between devices with their start and end apart: 1 -> 0, of which waited for: 1 -> 0; matrix products, arithmetic and copies ran while one was open for 0% -> 0% of each run, Pallas kernels for 0% -> 0%
where the time goes in v1:
time: 31.4 us; the launch traced here: 31.2 us
  Pallas kernels  27.1 us (86%)
  local copies, waits for them, and re-layouts  4.09 us (13%)
    pallas_call x1, Pallas kernels, per_device_grid(): pl.pallas_call(grid_kernel, out_shape=jax.ShapeDtypeStruct((rows, 16 * ro...  27.1 us
    unnamed x11, local copies, waits for them, and re-layouts  4.09 us

profile of v1, /device:TPU:0, one launch (start us, length us, event | category | flops | bytes accessed | tf_op | source)
XLA Modules:
  0.0 31.2 jit_solution(18361550887240940980)
XLA Ops:
  0.0 0.0 copy-start.3
  0.0 0.0 copy-start.4
  0.0 0.7 %copy-done.3 = s32[32]{0:T(128)S(1)} copy-done((s32[32]{0:T(128)S(1)}, s32[32]{0:T(128)}, u32[]{:S(2)}) %copy-start.3) | copy-done | bytes 152
  0.7 0.0 copy-done.4
  0.7 0.0 copy-start
  0.7 0.9 %copy-done = bf16[32,4096]{1,0:T(8,128)(2,1)S(1)} copy-done((bf16[32,4096]{1,0:T(8,128)(2,1)S(1)}, bf16[32,4096]{1,0:T(8,128)(2,1)}, u32[]{:S(2)}) %copy-start) | copy-done | bytes 262168
  1.6 0.0 copy-start.1
  1.6 0.9 %copy-done.1 = bf16[32,4096]{1,0:T(8,128)(2,1)S(1)} copy-done((bf16[32,4096]{1,0:T(8,128)(2,1)S(1)}, bf16[32,4096]{1,0:T(8,128)(2,1)}, u32[]{:S(2)}) %copy-start.1) | copy-done | bytes 262168
  2.6 0.0 copy-start.2
  2.6 0.9 %copy-done.2 = f32[8,4096]{1,0:T(8,128)S(1)} copy-done((f32[8,4096]{1,0:T(8,128)S(1)}, f32[8,4096]{1,0:T(8,128)}, u32[]{:S(2)}) %copy-start.2) | copy-done | bytes 131096
  3.5 27.1 %shard_map.55 = bf16[32,512]{1,0:T(8,128)(2,1)S(1)} custom-call(bf16[32,4096]{1,0:T(8,128)(2,1)S(1)} %copy-done, bf16[32,4096]{1,0:T(8,128)(2,1)S(1)} %copy-done.1, s32[1,32]{1,0:T(1,128)S(1)} %bitcast.2, f32[8,4096]{1,0:T(8,128)S(1)} %copy-done.2, f32[1,32]{1,0:T(1,128)S(1)} %bitcast.3), custom_call_target="tpu_custom_call" | custom-call | tf_op jit(solution)/shard_map/pallas_call | solution.py:268
  30.6 0.6 %copy.7 = bf16[32,512]{1,0:T(8,128)(2,1)} copy(bf16[32,512]{1,0:T(8,128)(2,1)S(1)} %shard_map.55) | data formatting | bytes 65536
Async XLA Ops:
  0.0 0.7 %copy-start.3 = (s32[32]{0:T(128)S(1)}, s32[32]{0:T(128)}, u32[]{:S(2)}) copy-start(s32[32]{0:T(128)} %param.7) | copy-start | bytes 388
  0.0 0.7 %copy-start.4 = (f32[32]{0:T(128)S(1)}, f32[32]{0:T(128)}, u32[]{:S(2)}) copy-start(f32[32]{0:T(128)} %param.9) | copy-start | bytes 388
  0.7 0.9 %copy-start = (bf16[32,4096]{1,0:T(8,128)(2,1)S(1)}, bf16[32,4096]{1,0:T(8,128)(2,1)}, u32[]{:S(2)}) copy-start(bf16[32,4096]{1,0:T(8,128)(2,1)} %left.1) | copy-start | bytes 786436
  1.6 0.9 %copy-start.1 = (bf16[32,4096]{1,0:T(8,128)(2,1)S(1)}, bf16[32,4096]{1,0:T(8,128)(2,1)}, u32[]{:S(2)}) copy-start(bf16[32,4096]{1,0:T(8,128)(2,1)} %band.1) | copy-start | bytes 786436
  2.6 0.9 %copy-start.2 = (f32[8,4096]{1,0:T(8,128)S(1)}, f32[8,4096]{1,0:T(8,128)}, u32[]{:S(2)}) copy-start(f32[8,4096]{1,0:T(8,128)} %radial.1) | copy-start | bytes 393220

commit v2 on v1

--- a/solution.py
+++ b/solution.py
@@ -38,8 +38,8 @@
 
 def grid_kernel(
     left, band, mult, radial, green, out,
-    lbuf, bbuf, rbuf, info, infobuf, psend, precv, msg, outbuf,
-    rsem, lsem, bsem, isem, psem, osem, lsend, bsend, isend, osend,
+    lbuf, bbuf, rbuf, info, infoin, infobuf, psend, precv, msg, outbuf,
+    rsem, lsem, bsem, isem, psem, osem, lsend, bsend, isend, osend, know,
 ):
     e = lax.axis_index("energy")
     k = lax.axis_index("kpt")
@@ -50,12 +50,13 @@
     own = k % 4
 
     barrier = pltpu.get_barrier_semaphore()
-    for de in range(2):
-        for dk in range(16):
-            if de or dk:
-                pl.semaphore_signal(
-                    barrier, inc=1, device_id=((e + de) % 2, (k + dk) % 16), device_id_type=MESH
-                )
+    across_y = (1 - e, k)
+    for target in (
+        [(e, 4 * ((z + dz) % 4) + 2 * x + e) for dz in (1, 2, 3)]
+        + [(e, 4 * z + 2 * (1 - x) + dc) for dc in range(2)]
+        + [(e, 4 * z + 2 * x + 1 - c), across_y]
+    ):
+        pl.semaphore_signal(barrier, inc=1, device_id=target, device_id_type=MESH)
 
     def cols(core, n):
         return pl.ds(pl.multiple_of(core * half + n * step, 128), step)
@@ -82,36 +83,39 @@
                 band.at[:, cols(c, n)], bbuf.at[slot(z), at(n)], bsem.at[z, n]
             ).start()
 
+    row = lax.broadcasted_iota(jnp.int32, info.shape, 0)
     info[...] = jnp.zeros_like(info)
     info[0:1, 0:rows] = green[...]
-    info[1:2, 0:rows] = mult[...].astype(jnp.float32)
+    info[1:2, 0:rows] = green[...]
+    info[2:3, 0:rows] = mult[...].astype(jnp.float32)
     info[...] = pltpu.roll(info[...], z * rows, 1)
 
-    pl.semaphore_wait(barrier, 31)
+    @pl.when(c == e)
+    def _():
+        pl.semaphore_wait(barrier, 10)
+
+    @pl.when(c != e)
+    def _():
+        pl.semaphore_wait(barrier, 4)
+
+    info_over = pltpu.make_async_remote_copy(
+        src_ref=info, dst_ref=infoin, send_sem=isend.at[7], recv_sem=isend.at[8],
+        device_id=across_y, device_id_type=MESH,
+    )
+
+    @pl.when(c != e)
+    def _():
+        info_over.start()
 
     sends = []
-    for dz in range(4):
-        for dc in range(2):
-            target = (c, ((z + dz) % 4) * 4 + 2 * x + (c + dc) % 2)
-            copy = pltpu.make_async_remote_copy(
-                src_ref=info, dst_ref=infobuf.at[e, z], send_sem=isend.at[dz * 2 + dc],
-                recv_sem=isem.at[e, z], device_id=target, device_id_type=MESH,
-            )
-            if dz or dc:
-                copy.start()
-                sends.append(copy)
-            else:
-                own_info = copy
-    info_local = pltpu.make_async_copy(info, infobuf.at[e, z], isem.at[e, z])
-
-    @pl.when(c == e)
-    def _():
-        info_local.start()
-
-    @pl.when(c != e)
-    def _():
-        own_info.start()
-
+    info_sends = [
+        pltpu.make_async_remote_copy(
+            src_ref=infobuf.at[z], dst_ref=infobuf.at[z], send_sem=isend.at[i],
+            recv_sem=isem.at[z], device_id=(e, ((z + dz) % 4) * 4 + 2 * x + (c + dc) % 2),
+            device_id_type=MESH,
+        )
+        for i, (dz, dc) in enumerate(((1, 0), (1, 1), (2, 0), (2, 1), (3, 0), (3, 1), (0, 1)))
+    ]
     band_sends = []
     for n in range(CHUNKS):
         for i, (dx, dc) in enumerate(((1, 0), (1, 1), (0, 1))):
@@ -133,10 +137,23 @@
                 )
             )
 
-    @pl.when(c == e)
-    def _():
-        for copy in band_sends:
-            copy.start()
+        @pl.when(c == e)
+        def _():
+            for copy in band_sends[n * 7:]:
+                copy.start()
+            if n == 0:
+                info_over.wait_recv()
+                infobuf[z] = jnp.where(row == 1 - e, infoin[...], info[...])
+                for copy in info_sends:
+                    copy.start()
+
+    @pl.when(c == e)
+    def _():
+        pl.semaphore_signal(
+            know, inc=1, device_id=(e, 4 * z + 2 * (1 - x) + c), device_id_type=MESH
+        )
+        pl.semaphore_wait(know, 1)
+        pl.semaphore_signal(know, inc=1, device_id=across_y, device_id_type=MESH)
 
     radial_copy.wait()
     whole = rbuf[...]
@@ -148,21 +165,26 @@
         [high.astype(jnp.float32), middle.astype(jnp.float32), low, jnp.zeros_like(low)], axis=0
     ).astype(jnp.bfloat16)
 
-    for energy in range(2):
-        for zz in range(4):
-            pltpu.make_async_copy(info, infobuf.at[energy, zz], isem.at[energy, zz]).wait()
-    data = [infobuf[i, 0] + infobuf[i, 1] + infobuf[i, 2] + infobuf[i, 3] for i in range(2)]
+    for i in (1, 2, 3):
+        other_z = (z + i) % 4
+        pltpu.make_async_copy(info, infobuf.at[other_z], isem.at[other_z]).wait()
+
+    @pl.when(c != e)
+    def _():
+        pltpu.make_async_copy(info, infobuf.at[z], isem.at[z]).wait()
+
+    data = infobuf[0] + infobuf[1] + infobuf[2] + infobuf[3]
     lanes = 4 * rows
     down = lax.broadcasted_iota(jnp.int32, (lanes, lanes), 0)
     across = lax.broadcasted_iota(jnp.int32, (lanes, lanes), 1)
     scale = [
-        jnp.sum(jnp.where(down == across, data[i][0:1, :], 0.0), axis=1, keepdims=True)
+        jnp.sum(jnp.where(down == across, data[i:i + 1, :], 0.0), axis=1, keepdims=True)
         for i in range(2)
     ]
     first = c == 0
     mine = jnp.where(first, scale[0], scale[1])
     other = jnp.where(first, scale[1], scale[0])
-    level = jnp.sum(jnp.where(down == across, data[0][1:2, :], 0.0), axis=1, keepdims=True)
+    level = jnp.sum(jnp.where(down == across, data[2:3, :], 0.0), axis=1, keepdims=True)
     place = lax.broadcasted_iota(jnp.int32, (lanes, 4 * LMAX), 1)
     onehot = jnp.where(
         jnp.logical_and((place % LMAX).astype(jnp.float32) == level, place < 3 * LMAX), 1.0, 0.0
@@ -203,6 +225,10 @@
     finished = (total[:, lanes:] + precv[...]).astype(jnp.bfloat16)
     cyclic = jnp.dot(order, finished, preferred_element_type=jnp.float32)
     msg[...] = cyclic.reshape(msg.shape)
+
+    @pl.when(c != e)
+    def _():
+        pl.semaphore_wait(know, 1)
 
     for dq in range(16):
         q = (k + dq) % 16
@@ -250,12 +276,12 @@
 
     @pl.when(c == e)
     def _():
-        for copy in band_sends:
+        for copy in band_sends + info_sends:
             copy.wait_send()
 
     @pl.when(c != e)
     def _():
-        own_info.wait_send()
+        info_over.wait_send()
         own_out.wait_send()
 
 
@@ -275,16 +301,18 @@
             pltpu.VMEM((lanes, half), jnp.bfloat16),
             pltpu.VMEM((LMAX, half), jnp.float32),
             pltpu.VMEM((8, lanes), jnp.float32),
-            pltpu.VMEM((2, 4, 8, lanes), jnp.float32),
+            pltpu.VMEM((8, lanes), jnp.float32),
+            pltpu.VMEM((4, 8, lanes), jnp.float32),
             pltpu.VMEM((lanes, lanes), jnp.float32),
             pltpu.VMEM((lanes, lanes), jnp.float32),
             pltpu.VMEM((16, 8, lanes), jnp.float32),
             pltpu.VMEM((4, 4, 8, lanes), jnp.float32),
-            dma, dma((4, CHUNKS)), dma((4, CHUNKS)), dma((2, 4)), dma((2,)), dma((4, 4)),
-            dma((3, CHUNKS)), dma((7, CHUNKS)), dma((8,)), dma((16,)),
+            dma, dma((4, CHUNKS)), dma((4, CHUNKS)), dma((4,)), dma((2,)), dma((4, 4)),
+            dma((3, CHUNKS)), dma((7, CHUNKS)), dma((9,)), dma((16,)),
+            pltpu.SemaphoreType.REGULAR,
         ],
         compiler_params=pltpu.CompilerParams(
-            collective_id=0, has_side_effects=True, vmem_limit_bytes=32 * 1024 * 1024
+            collective_id=0, has_side_effects=True, vmem_limit_bytes=60 * 1024 * 1024
         ),
     )(left_table, band_table, band_multipole.reshape(1, rows), radial_weight, green_weight.reshape(1, rows))
 

time: 31.4 us -> 29 us (0.924)
  local copies, waits for them, and re-layouts: 4.09 us -> 1.38 us
    unnamed x11 -> x1, local copies, waits for them, and re-layouts: 4.09 us -> 1.38 us
where the time goes in v2:
time: 29 us; the launch traced here: 28.8 us
  Pallas kernels  27.4 us (94%)
  local copies, waits for them, and re-layouts  1.38 us (5%)
    pallas_call x1, Pallas kernels, per_device_grid(): pl.pallas_call(grid_kernel, out_shape=jax.ShapeDtypeStruct((rows, 16 * ro...  27.4 us
    unnamed x1, local copies, waits for them, and re-layouts  1.38 us

profile of v2, /device:TPU:0, one launch (start us, length us, event | category | flops | bytes accessed | tf_op | source)
XLA Modules:
  0.0 28.8 jit_solution(12616494507917132616)
XLA Ops:
  0.0 27.4 %shard_map.55 = bf16[32,512]{1,0:T(8,128)(2,1)} custom-call(bf16[32,4096]{1,0:T(8,128)(2,1)} %left.1, bf16[32,4096]{1,0:T(8,128)(2,1)} %band.1, s32[1,32]{1,0:T(1,128)} %bitcast.2, f32[8,4096]{1,0:T(8,128)} %radial.1, f32[1,32]{1,0:T(1,128)} %bitcast.3), custom_call_target="tpu_custom_call" | custom-call | tf_op jit(solution)/shard_map/pallas_call | solution.py:294
  27.4 1.4 %copy.7 = bf16[32,512]{1,0:T(8,128)(2,1)} copy(bf16[32,512]{1,0:T(8,128)(2,1)} %shard_map.55) | data formatting | bytes 65536

commit v3 on v2

--- a/solution.py
+++ b/solution.py
@@ -10,6 +10,7 @@
 LMAX = 8
 MESH = pl.DeviceIdType.MESH
 CHUNKS = 4
+BAND_ORDER = ((2, 0), (2, 1), (1, 0), (1, 1), (3, 0), (3, 1), (0, 1))
 
 
 def build_part(left_table, band_part):
@@ -39,7 +40,7 @@
 def grid_kernel(
     left, band, mult, radial, green, out,
     lbuf, bbuf, rbuf, info, infoin, infobuf, psend, precv, msg, outbuf,
-    rsem, lsem, bsem, isem, psem, osem, lsend, bsend, isend, osend, know,
+    rsem, lsem, bsem, isem, psem, osem, lsend, bsend, isend, osend, fsend, know,
 ):
     e = lax.axis_index("energy")
     k = lax.axis_index("kpt")
@@ -116,7 +117,25 @@
         )
         for i, (dz, dc) in enumerate(((1, 0), (1, 1), (2, 0), (2, 1), (3, 0), (3, 1), (0, 1)))
     ]
+    inner = jnp.logical_or(z == 1, z == 2)
+    far = jnp.where(z >= 2, 0, 3)
+    relays = [
+        pltpu.make_async_remote_copy(
+            src_ref=bbuf.at[slot(far), at(n)], dst_ref=bbuf.at[slot(far), at(n)],
+            send_sem=fsend.at[n], recv_sem=bsem.at[far, n],
+            device_id=(e, 4 * (3 - far) + 2 * x + c), device_id_type=MESH,
+        )
+        for n in range(CHUNKS)
+    ]
     band_sends = []
+
+    def direct(n, act):
+        for copy, (dz, _) in zip(band_sends[n * 7:n * 7 + 7], BAND_ORDER):
+            if dz in (0, 2):
+                act(copy)
+            else:
+                pl.when(z != (3 if dz == 1 else 0))(functools.partial(act, copy))
+
     for n in range(CHUNKS):
         for i, (dx, dc) in enumerate(((1, 0), (1, 1), (0, 1))):
             core = (c + dc) % 2
@@ -127,7 +146,7 @@
             )
             copy.start()
             sends.append(copy)
-        for i, (dz, dc) in enumerate(((1, 0), (1, 1), (2, 0), (2, 1), (3, 0), (3, 1), (0, 1))):
+        for i, (dz, dc) in enumerate(BAND_ORDER):
             core = (c + dc) % 2
             band_sends.append(
                 pltpu.make_async_remote_copy(
@@ -139,8 +158,7 @@
 
         @pl.when(c == e)
         def _():
-            for copy in band_sends[n * 7:]:
-                copy.start()
+            direct(n, lambda copy: copy.start())
             if n == 0:
                 info_over.wait_recv()
                 infobuf[z] = jnp.where(row == 1 - e, infoin[...], info[...])
@@ -190,18 +208,24 @@
         jnp.logical_and((place % LMAX).astype(jnp.float32) == level, place < 3 * LMAX), 1.0, 0.0
     ).astype(jnp.bfloat16)
 
+    def band_wait(i, n):
+        pltpu.make_async_copy(
+            bbuf.at[slot(i), at(n)], bbuf.at[slot(i), at(n)], bsem.at[i, n]
+        ).wait()
+
     total = jnp.zeros((lanes, 2 * lanes), jnp.float32)
     for n in range(CHUNKS):
         picked = jnp.dot(
             onehot, terms[:, n * step:(n + 1) * step], preferred_element_type=jnp.float32
         )
+        band_wait(far, n)
+        pl.when(inner)(relays[n].start)
         for i in range(4):
             pltpu.make_async_copy(
                 lbuf.at[slot(i), at(n)], lbuf.at[slot(i), at(n)], lsem.at[i, n]
             ).wait()
-            pltpu.make_async_copy(
-                bbuf.at[slot(i), at(n)], bbuf.at[slot(i), at(n)], bsem.at[i, n]
-            ).wait()
+        for i in (1, 2, 3):
+            band_wait((far + i) % 4, n)
         product = bbuf[:, n * step:(n + 1) * step].astype(jnp.float32) * picked
         weighted = jnp.concatenate(
             [(product * other).astype(jnp.bfloat16), (product * mine).astype(jnp.bfloat16)], axis=0
@@ -276,7 +300,14 @@
 
     @pl.when(c == e)
     def _():
-        for copy in band_sends + info_sends:
+        for copy in info_sends:
+            copy.wait_send()
+        for n in range(CHUNKS):
+            direct(n, lambda copy: copy.wait_send())
+
+    @pl.when(inner)
+    def _():
+        for copy in relays:
             copy.wait_send()
 
     @pl.when(c != e)
@@ -308,7 +339,7 @@
             pltpu.VMEM((16, 8, lanes), jnp.float32),
             pltpu.VMEM((4, 4, 8, lanes), jnp.float32),
             dma, dma((4, CHUNKS)), dma((4, CHUNKS)), dma((4,)), dma((2,)), dma((4, 4)),
-            dma((3, CHUNKS)), dma((7, CHUNKS)), dma((9,)), dma((16,)),
+            dma((3, CHUNKS)), dma((7, CHUNKS)), dma((9,)), dma((16,)), dma((CHUNKS,)),
             pltpu.SemaphoreType.REGULAR,
         ],
         compiler_params=pltpu.CompilerParams(

time: 29 us -> 27.2 us (0.938)
  Pallas kernels: 27.4 us -> 25.7 us
    pallas_call x1, Pallas kernels: 27.4 us -> 25.7 us  [per_device_grid(): pl.pallas_call(grid_kernel, out_shape=jax.ShapeDtypeStruct((rows, 16 * ro...]
where the time goes in v3:
time: 27.2 us; the launch traced here: 27.1 us
  Pallas kernels  25.7 us (94%)
  local copies, waits for them, and re-layouts  1.38 us (5%)
    pallas_call x1, Pallas kernels, per_device_grid(): pl.pallas_call(grid_kernel, out_shape=jax.ShapeDtypeStruct((rows, 16 * ro...  25.7 us
    unnamed x1, local copies, waits for them, and re-layouts  1.38 us

profile of v3, /device:TPU:0, one launch (start us, length us, event | category | flops | bytes accessed | tf_op | source)
XLA Modules:
  0.0 27.1 jit_solution(14262459097470522560)
XLA Ops:
  0.0 25.7 %shard_map.55 = bf16[32,512]{1,0:T(8,128)(2,1)} custom-call(bf16[32,4096]{1,0:T(8,128)(2,1)} %left.1, bf16[32,4096]{1,0:T(8,128)(2,1)} %band.1, s32[1,32]{1,0:T(1,128)} %bitcast.2, f32[8,4096]{1,0:T(8,128)} %radial.1, f32[1,32]{1,0:T(1,128)} %bitcast.3), custom_call_target="tpu_custom_call" | custom-call | tf_op jit(solution)/shard_map/pallas_call | solution.py:325
  25.7 1.4 %copy.7 = bf16[32,512]{1,0:T(8,128)(2,1)} copy(bf16[32,512]{1,0:T(8,128)(2,1)} %shard_map.55) | data formatting | bytes 65536

commit v4 on v3

--- a/solution.py
+++ b/solution.py
@@ -52,9 +52,22 @@
 
     barrier = pltpu.get_barrier_semaphore()
     across_y = (1 - e, k)
+    inner = jnp.logical_or(z == 1, z == 2)
+    far = jnp.where(z >= 2, 0, 3)
+
+    def beside_ends(dz, act):
+        if dz in (0, 2):
+            act()
+        else:
+            pl.when(z != (3 if dz == 1 else 0))(act)
+
+    for dz in (2, 1, 3):
+        beside_ends(dz, functools.partial(
+            pl.semaphore_signal, barrier, inc=1,
+            device_id=(e, 4 * ((z + dz) % 4) + 2 * x + e), device_id_type=MESH,
+        ))
     for target in (
-        [(e, 4 * ((z + dz) % 4) + 2 * x + e) for dz in (1, 2, 3)]
-        + [(e, 4 * z + 2 * (1 - x) + dc) for dc in range(2)]
+        [(e, 4 * z + 2 * (1 - x) + dc) for dc in range(2)]
         + [(e, 4 * z + 2 * x + 1 - c), across_y]
     ):
         pl.semaphore_signal(barrier, inc=1, device_id=target, device_id_type=MESH)
@@ -91,9 +104,13 @@
     info[2:3, 0:rows] = mult[...].astype(jnp.float32)
     info[...] = pltpu.roll(info[...], z * rows, 1)
 
-    @pl.when(c == e)
+    @pl.when(jnp.logical_and(c == e, inner))
     def _():
         pl.semaphore_wait(barrier, 10)
+
+    @pl.when(jnp.logical_and(c == e, jnp.logical_not(inner)))
+    def _():
+        pl.semaphore_wait(barrier, 8)
 
     @pl.when(c != e)
     def _():
@@ -117,8 +134,10 @@
         )
         for i, (dz, dc) in enumerate(((1, 0), (1, 1), (2, 0), (2, 1), (3, 0), (3, 1), (0, 1)))
     ]
-    inner = jnp.logical_or(z == 1, z == 2)
-    far = jnp.where(z >= 2, 0, 3)
+    info_relay = pltpu.make_async_remote_copy(
+        src_ref=infobuf.at[far], dst_ref=infobuf.at[far], send_sem=isend.at[9],
+        recv_sem=isem.at[far], device_id=(e, 4 * (3 - far) + 2 * x + c), device_id_type=MESH,
+    )
     relays = [
         pltpu.make_async_remote_copy(
             src_ref=bbuf.at[slot(far), at(n)], dst_ref=bbuf.at[slot(far), at(n)],
@@ -131,10 +150,11 @@
 
     def direct(n, act):
         for copy, (dz, _) in zip(band_sends[n * 7:n * 7 + 7], BAND_ORDER):
-            if dz in (0, 2):
-                act(copy)
-            else:
-                pl.when(z != (3 if dz == 1 else 0))(functools.partial(act, copy))
+            beside_ends(dz, functools.partial(act, copy))
+
+    def tell(act):
+        for copy, dz in zip(info_sends, (1, 1, 2, 2, 3, 3, 0)):
+            beside_ends(dz, functools.partial(act, copy))
 
     for n in range(CHUNKS):
         for i, (dx, dc) in enumerate(((1, 0), (1, 1), (0, 1))):
@@ -162,16 +182,7 @@
             if n == 0:
                 info_over.wait_recv()
                 infobuf[z] = jnp.where(row == 1 - e, infoin[...], info[...])
-                for copy in info_sends:
-                    copy.start()
-
-    @pl.when(c == e)
-    def _():
-        pl.semaphore_signal(
-            know, inc=1, device_id=(e, 4 * z + 2 * (1 - x) + c), device_id_type=MESH
-        )
-        pl.semaphore_wait(know, 1)
-        pl.semaphore_signal(know, inc=1, device_id=across_y, device_id_type=MESH)
+                tell(lambda copy: copy.start())
 
     radial_copy.wait()
     whole = rbuf[...]
@@ -183,14 +194,17 @@
         [high.astype(jnp.float32), middle.astype(jnp.float32), low, jnp.zeros_like(low)], axis=0
     ).astype(jnp.bfloat16)
 
-    for i in (1, 2, 3):
-        other_z = (z + i) % 4
-        pltpu.make_async_copy(info, infobuf.at[other_z], isem.at[other_z]).wait()
-
-    @pl.when(c != e)
-    def _():
-        pltpu.make_async_copy(info, infobuf.at[z], isem.at[z]).wait()
-
+    def info_wait(i):
+        pltpu.make_async_copy(info, infobuf.at[i], isem.at[i]).wait()
+
+    @pl.when(c != e)
+    def _():
+        info_wait(z)
+
+    info_wait(far)
+    pl.when(inner)(info_relay.start)
+    info_wait(jnp.where(inner, 3 - far, 1))
+    info_wait(jnp.where(inner, 3 - z, 2))
     data = infobuf[0] + infobuf[1] + infobuf[2] + infobuf[3]
     lanes = 4 * rows
     down = lax.broadcasted_iota(jnp.int32, (lanes, lanes), 0)
@@ -226,6 +240,15 @@
             ).wait()
         for i in (1, 2, 3):
             band_wait((far + i) % 4, n)
+        if n == 0:
+            @pl.when(c == e)
+            def _():
+                pl.semaphore_signal(
+                    know, inc=1, device_id=(e, 4 * z + 2 * (1 - x) + c), device_id_type=MESH
+                )
+                pl.semaphore_wait(know, 1)
+                pl.semaphore_signal(know, inc=1, device_id=across_y, device_id_type=MESH)
+
         product = bbuf[:, n * step:(n + 1) * step].astype(jnp.float32) * picked
         weighted = jnp.concatenate(
             [(product * other).astype(jnp.bfloat16), (product * mine).astype(jnp.bfloat16)], axis=0
@@ -300,13 +323,13 @@
 
     @pl.when(c == e)
     def _():
-        for copy in info_sends:
-            copy.wait_send()
+        tell(lambda copy: copy.wait_send())
         for n in range(CHUNKS):
             direct(n, lambda copy: copy.wait_send())
 
     @pl.when(inner)
     def _():
+        info_relay.wait_send()
         for copy in relays:
             copy.wait_send()
 
@@ -339,7 +362,7 @@
             pltpu.VMEM((16, 8, lanes), jnp.float32),
             pltpu.VMEM((4, 4, 8, lanes), jnp.float32),
             dma, dma((4, CHUNKS)), dma((4, CHUNKS)), dma((4,)), dma((2,)), dma((4, 4)),
-            dma((3, CHUNKS)), dma((7, CHUNKS)), dma((9,)), dma((16,)), dma((CHUNKS,)),
+            dma((3, CHUNKS)), dma((7, CHUNKS)), dma((10,)), dma((16,)), dma((CHUNKS,)),
             pltpu.SemaphoreType.REGULAR,
         ],
         compiler_params=pltpu.CompilerParams(

time: 27.2 us -> 27 us (level)
  no operation moved by 1% of the time
where the time goes in v4:
time: 27 us; the launch traced here: 26.9 us
  Pallas kernels  25.5 us (94%)
  local copies, waits for them, and re-layouts  1.38 us (5%)
    pallas_call x1, Pallas kernels, per_device_grid(): pl.pallas_call(grid_kernel, out_shape=jax.ShapeDtypeStruct((rows, 16 * ro...  25.5 us
    unnamed x1, local copies, waits for them, and re-layouts  1.38 us

profile of v4, /device:TPU:0, one launch (start us, length us, event | category | flops | bytes accessed | tf_op | source)
XLA Modules:
  0.0 26.9 jit_solution(17356155780999335356)
XLA Ops:
  0.0 25.5 %shard_map.55 = bf16[32,512]{1,0:T(8,128)(2,1)} custom-call(bf16[32,4096]{1,0:T(8,128)(2,1)} %left.1, bf16[32,4096]{1,0:T(8,128)(2,1)} %band.1, s32[1,32]{1,0:T(1,128)} %bitcast.2, f32[8,4096]{1,0:T(8,128)} %radial.1, f32[1,32]{1,0:T(1,128)} %bitcast.3), custom_call_target="tpu_custom_call" | custom-call | tf_op jit(solution)/shard_map/pallas_call | solution.py:348
  25.5 1.4 %copy.7 = bf16[32,512]{1,0:T(8,128)(2,1)} copy(bf16[32,512]{1,0:T(8,128)(2,1)} %shard_map.55) | data formatting | bytes 65536
